TPU v7x, 512 devices: a whole 4x4x16 slice. The times are simulated.
512 devices in a mesh: group: 8 (over y_lo, x), member: 64 (over z, y_hi, core).
Axes of the slice: x: 4, y: 4 (y_hi: 2, y_lo: 2; y = y_hi * 2 + y_lo), z: 16, core: 2. Of those that a mesh axis runs over, the one named last changes fastest.
Arguments:
- grads: bfloat16 [1, 131072, 1024], P(None, ('group', 'member')), may hold values from -3000 to 3000
- member_partner: int32 [64], replicated, may hold values from 0 to 63, as said below
- group_partner: int32 [512], replicated, may hold values from 0 to 511, as said below
Outputs:
- tiles: float32 [2, 131072, 256], P(None, ('group', 'member'))
- self_scores: float32 [131072], P(('group', 'member'))
Inputs may be any that keep to these rules, and one draw needn't show every extreme that they name: Pairs the blocks of a group: member_partner[member_partner[m]] == m and member_partner[m] != m. Pairs the blocks: group_partner[group_partner[b]] == b; all blocks of group g are paired with blocks of one other group, the same for all of g's blocks, each block of that group once.
All inputs are finite; a program needn't handle non-finite values.
Results may differ from a plain program's by a relative error of at most 0.0047.
Values may be sent and summed in bfloat16 or wider, within the bound.
A program may use at most 128 MiB of HBM per device.

v0:
```python
import math

import jax
import jax.numpy as jnp
from jax import lax
from jax.sharding import PartitionSpec as P

DAMP = 1.0


def precondition(block, chol):
    right = block.astype(jnp.float32).T
    half = jax.scipy.linalg.solve_triangular(chol, right, lower=True)
    whole = jax.scipy.linalg.solve_triangular(chol, half, lower=True, trans=1)
    return whole.T.astype(jnp.bfloat16)


def apply_all(blocks, chols):
    return jnp.stack([precondition(blocks[0], chols[0])])


def gram_tile(left, right, scale):
    return jnp.einsum("lrk,lsk->rs", left, right, preferred_element_type=jnp.float32) * scale


def pack_terms(local):
    return local.reshape(-1)


def unpack_terms(flat, width):
    return flat.reshape(width, width)


def per_device(grads, member_partner, group_partner):
    layers, rows, width = grads.shape
    members = lax.axis_size("member")
    groups = lax.axis_size("group")
    total_rows = rows * members * groups
    eye = jnp.eye(width, dtype=jnp.float32)
    block = grads[0]
    local = lax.dot_general(
        block, block, (((0,), (0,)), ((), ())), preferred_element_type=jnp.float32
    )
    flat = pack_terms(local)
    summed = lax.psum(flat, ("group", "member"))
    fisher = unpack_terms(summed, width)
    chols = [jnp.linalg.cholesky(fisher / total_rows + DAMP * eye)]
    precond = apply_all(grads, chols)
    self_scores = jnp.sum(precond.astype(jnp.float32) * grads.astype(jnp.float32), axis=(0, 2)) / (
        layers * width
    )
    scale = 1.0 / math.sqrt(layers * width)
    member_here = lax.axis_index("member")
    group_here = lax.axis_index("group")
    block_here = group_here * members + member_here
    below_member = member_here < member_partner[member_here]
    below_group = block_here < group_partner[block_here]
    partner_groups = group_partner[jnp.arange(groups, dtype=jnp.int32) * members] // members
    other_group_here = partner_groups[group_here]
    source_members = (
        group_partner[other_group_here * members + jnp.arange(members, dtype=jnp.int32)] % members
    )
    outgoing_member = jnp.where(below_member, precond, grads)
    outgoing_group = jnp.where(below_group, precond, grads)
    pieces = outgoing_member.reshape(layers, members, rows // members, width)
    arrived = lax.all_to_all(pieces, "member", split_axis=1, concat_axis=1, tiled=True)
    arrived = jnp.take(arrived, member_partner, axis=1)
    partner_member = lax.all_to_all(
        arrived, "member", split_axis=1, concat_axis=1, tiled=True
    ).reshape(layers, rows, width)
    pieces = outgoing_group.reshape(layers, members, rows // members, width)
    arrived = lax.all_to_all(pieces, "member", split_axis=1, concat_axis=1, tiled=True)
    arrived = jnp.take(arrived, source_members, axis=1)
    sectioned = lax.all_to_all(arrived, "member", split_axis=1, concat_axis=1, tiled=True).reshape(
        layers, rows, width
    )
    pieces = sectioned.reshape(layers, groups, rows // groups, width)
    arrived = lax.all_to_all(pieces, "group", split_axis=1, concat_axis=1, tiled=True)
    arrived = jnp.take(arrived, partner_groups, axis=1)
    partner_group = lax.all_to_all(
        arrived, "group", split_axis=1, concat_axis=1, tiled=True
    ).reshape(layers, rows, width)
    own_member = jnp.where(below_member, precond, grads)
    own_group = jnp.where(below_group, precond, grads)
    first_tile = gram_tile(own_member, partner_member, scale)
    second_tile = gram_tile(own_group, partner_group, scale)
    tiles = jnp.stack([first_tile, second_tile])
    return (tiles, self_scores)


def solution(mesh):
    return jax.shard_map(
        per_device,
        mesh=mesh,
        in_specs=(P(None, ("group", "member"), None), P(), P()),
        out_specs=(P(None, ("group", "member"), None), P(("group", "member"))),
        check_vma=False,
    )
```

profile of v0, /device:TPU:1, one launch (start us, length us, event | category | flops | bytes accessed | tf_op | source)
XLA Modules:
  0.0 1070.0 jit_solution(6841593655789287167)
XLA Ops:
  16.0 490.5 %all-reduce.3.cloned.1.call-done = f32[1048576]{0:T(1024)} async-done(((f32[1048576]{0:T(1024)}), f32[1048576]{0:T(1024)}) %all-reduce.3.cloned.1.call-update) | async-done | bytes 4194320 | tf_op jit(solution)/shard_map/psum | solution.py:45
  537.9 11.7 %cholesky.223 = f32[128,128]{1,0:T(8,128)S(1)} custom-call(f32[128,128]{1,0:T(8,128)S(1)} %cholesky.580), custom_call_target="Cholesky" | custom-call | tf_op jit(solution)/shard_map/jit(cholesky)/cholesky | solution.py:47
  549.7 9.8 custom-call.66
  565.9 11.9 %cholesky.244 = f32[128,128]{1,0:T(8,128)S(1)} custom-call(f32[128,128]{1,0:T(8,128)S(1)} %cholesky.584), custom_call_target="Cholesky" | custom-call | tf_op jit(solution)/shard_map/jit(cholesky)/cholesky | solution.py:47
  578.5 9.8 custom-call.67
  591.7 11.7 %cholesky.468 = f32[128,128]{1,0:T(8,128)S(1)} custom-call(f32[128,128]{1,0:T(8,128)S(1)} %cholesky.589), custom_call_target="Cholesky" | custom-call | tf_op jit(solution)/shard_map/jit(cholesky)/cholesky | solution.py:47
  604.6 9.8 custom-call.68
  618.0 12.1 %cholesky.487 = f32[128,128]{1,0:T(8,128)S(1)} custom-call(f32[128,128]{1,0:T(8,128)S(1)} %cholesky.594), custom_call_target="Cholesky" | custom-call | tf_op jit(solution)/shard_map/jit(cholesky)/cholesky | solution.py:47
  631.4 9.8 custom-call.69
  644.7 11.7 %cholesky.506 = f32[128,128]{1,0:T(8,128)S(1)} custom-call(f32[128,128]{1,0:T(8,128)S(1)} %cholesky.599), custom_call_target="Cholesky" | custom-call | tf_op jit(solution)/shard_map/jit(cholesky)/cholesky | solution.py:47
  657.7 10.0 custom-call.70
  671.0 11.7 %cholesky.526 = f32[128,128]{1,0:T(8,128)S(1)} custom-call(f32[128,128]{1,0:T(8,128)S(1)} %cholesky.604), custom_call_target="Cholesky" | custom-call | tf_op jit(solution)/shard_map/jit(cholesky)/cholesky | solution.py:47
  683.9 9.8 custom-call.71
  696.8 11.9 %cholesky.546 = f32[128,128]{1,0:T(8,128)S(1)} custom-call(f32[128,128]{1,0:T(8,128)S(1)} %cholesky.609), custom_call_target="Cholesky" | custom-call | tf_op jit(solution)/shard_map/jit(cholesky)/cholesky | solution.py:47
  709.9 9.8 custom-call.72
  722.3 11.7 %cholesky.564 = f32[128,128]{1,0:T(8,128)S(1)} custom-call(f32[128,128]{1,0:T(8,128)S(1)} %convolution_subtract_fusion.20), custom_call_target="Cholesky" | custom-call | tf_op jit(solution)/shard_map/jit(cholesky)/cholesky | solution.py:47
  745.7 23.0 %while.1 = (s32[]{:T(128)}, f32[1024,1024]{1,0:T(8,128)}, s32[8,2]{0,1:T(2,128)S(1)}, f32[8,128,128]{2,1,0:T(8,128)S(1)}, s32[]{:T(128)}) while((s32[]{:T(128)}, f32[1024,1024]{1,0:T(8,128)}, s32[8,2]{0,1:T(2,128)S(1)}, f32[8,128,128]{2,1,0:T(8,128)S(1)}, s32[]{:T(128)}) %tuple.65), condition=%wide.while_cond, body=%wide.while_body.sunk | while | flops 2 | bytes 131181 | solution.py:14
  768.6 79.0 %custom-call.73 = f32[8,128,128]{1,2,0:T(8,128)S(1)} custom-call(f32[8,128,128]{2,1,0:T(8,128)S(1)} %get-tuple-element.10), custom_call_target="InvertDiagBlocksLowerTriangular" | custom-call | tf_op jit(solution)/shard_map/jit(_solve_triangular)/triangular_solve | solution.py:14
  864.4 15.3 %all-to-all-start.2 = ((bf16[1,64,4,1024]{3,2,0,1:T(4,128)(2,1)}), bf16[1,64,4,1024]{3,2,0,1:T(4,128)(2,1)S(1)}, u32[]{:S(2)}, u32[]{:S(2)}) async-start(bf16[1,64,4,1024]{3,2,0,1:T(4,128)(2,1)} %bitcast.41), calls=%async_computation.2 | async-start | bytes 1048576 | tf_op jit(solution)/shard_map/all_to_all | solution.py:72
  882.5 31.1 %all-to-all-done.2 = bf16[1,64,4,1024]{3,2,0,1:T(4,128)(2,1)S(1)} async-done(((bf16[1,64,4,1024]{3,2,0,1:T(4,128)(2,1)}), bf16[1,64,4,1024]{3,2,0,1:T(4,128)(2,1)S(1)}, u32[]{:S(2)}, u32[]{:S(2)}) %all-to-all-start.2) | async-done | bytes 524320 | tf_op jit(solution)/shard_map/all_to_all | solution.py:72
  921.9 32.8 %all-to-all-done.3 = bf16[1,64,4,1024]{3,2,0,1:T(4,128)(2,1)S(1)} async-done(((bf16[1,64,4,1024]{3,2,0,1:T(4,128)(2,1)}), bf16[1,64,4,1024]{3,2,0,1:T(4,128)(2,1)S(1)}, u32[]{:S(2)}, u32[]{:S(2)}) %all-to-all-start.3) | async-done | bytes 524320 | tf_op jit(solution)/shard_map/all_to_all | solution.py:74
  960.6 33.1 %all-to-all-done = bf16[1,64,4,1024]{3,2,0,1:T(4,128)(2,1)S(1)} async-done(((bf16[1,64,4,1024]{3,2,0,1:T(4,128)(2,1)}), bf16[1,64,4,1024]{3,2,0,1:T(4,128)(2,1)S(1)}, u32[]{:S(2)}, u32[]{:S(2)}) %all-to-all-start) | async-done | bytes 524320 | tf_op jit(solution)/shard_map/all_to_all | solution.py:66
  1017.4 30.6 %all-to-all-done.1 = bf16[1,64,4,1024]{3,2,0,1:T(4,128)(2,1)S(1)} async-done(((bf16[1,64,4,1024]{3,2,0,1:T(4,128)(2,1)}), bf16[1,64,4,1024]{3,2,0,1:T(4,128)(2,1)S(1)}, u32[]{:S(2)}, u32[]{:S(2)}) %all-to-all-start.1) | async-done | bytes 524320 | tf_op jit(solution)/shard_map/all_to_all | solution.py:68
  1052.8 9.0 all-to-all-done.5
  (182 shorter events, 163.3 us)
Async XLA Ops:
  7.2 499.4 %all-reduce.3.cloned.1.call-start = ((), (), s32[]{:S(2)}) async-start(), calls=%async_computation.6 | async-start | bytes 8388608 | tf_op jit(solution)/shard_map/psum | solution.py:45
  12.1 1.0 copy-start.3
  12.1 1.3 copy-start
  12.1 2.5 copy-start.5
  536.0 1.9 copy-start.2
  847.7 5.0 copy-start.1
  864.4 49.2 %all-to-all-start.2 = ((bf16[1,64,4,1024]{3,2,0,1:T(4,128)(2,1)}), bf16[1,64,4,1024]{3,2,0,1:T(4,128)(2,1)S(1)}, u32[]{:S(2)}, u32[]{:S(2)}) async-start(bf16[1,64,4,1024]{3,2,0,1:T(4,128)(2,1)} %bitcast.41), calls=%async_computation.2 | async-start | bytes 1048576 | tf_op jit(solution)/shard_map/all_to_all | solution.py:72
  915.7 39.0 %all-to-all-start.3 = ((bf16[1,64,4,1024]{3,2,0,1:T(4,128)(2,1)}), bf16[1,64,4,1024]{3,2,0,1:T(4,128)(2,1)S(1)}, u32[]{:S(2)}, u32[]{:S(2)}) async-start(bf16[1,64,4,1024]{3,2,0,1:T(4,128)(2,1)} %fusion.25), calls=%async_computation.3 | async-start | bytes 1048576 | tf_op jit(solution)/shard_map/all_to_all | solution.py:74
  954.7 39.0 %all-to-all-start = ((bf16[1,64,4,1024]{3,2,0,1:T(4,128)(2,1)}), bf16[1,64,4,1024]{3,2,0,1:T(4,128)(2,1)S(1)}, u32[]{:S(2)}, u32[]{:S(2)}) async-start(bf16[1,64,4,1024]{3,2,0,1:T(4,128)(2,1)} %bitcast.211), calls=%async_computation | async-start | bytes 1048576 | tf_op jit(solution)/shard_map/all_to_all | solution.py:66
  993.6 0.8 copy-start.4
  994.4 13.8 %all-to-all-start.4 = ((bf16[1,8,32,1024]{3,2,0,1:T(8,128)(2,1)}), bf16[1,8,32,1024]{3,2,0,1:T(8,128)(2,1)S(1)}, u32[]{:S(2)}, u32[]{:S(2)}) async-start(bf16[1,8,32,1024]{3,2,0,1:T(8,128)(2,1)} %bitcast.210), calls=%async_computation.4 | async-start | bytes 1048576 | tf_op jit(solution)/shard_map/all_to_all | solution.py:78
  1008.2 39.9 %all-to-all-start.1 = ((bf16[1,64,4,1024]{3,2,0,1:T(4,128)(2,1)}), bf16[1,64,4,1024]{3,2,0,1:T(4,128)(2,1)S(1)}, u32[]{:S(2)}, u32[]{:S(2)}) async-start(bf16[1,64,4,1024]{3,2,0,1:T(4,128)(2,1)} %fusion.27), calls=%async_computation.1 | async-start | bytes 1048576 | tf_op jit(solution)/shard_map/all_to_all | solution.py:68
  1048.1 13.7 %all-to-all-start.5 = ((bf16[1,8,32,1024]{3,2,0,1:T(8,128)(2,1)}), bf16[1,8,32,1024]{3,2,0,1:T(8,128)(2,1)S(1)}, u32[]{:S(2)}, u32[]{:S(2)}) async-start(bf16[1,8,32,1024]{3,2,0,1:T(8,128)(2,1)} %fusion.24), calls=%async_computation.5 | async-start | bytes 1048576 | tf_op jit(solution)/shard_map/all_to_all | solution.py:80
Sparse Core Ops, SparseCore 0:
  13.4 493.0 all-reduce.2
where the time goes:
time: 1080 us; the launch traced here: 1070 us
  waiting for transfers between devices  634 us (59%)
  other arithmetic  276 us (26%)
  local copies, waits for them, and re-layouts  59.2 us (5%)
  matrix products  40.6 us (4%)
  starting transfers between devices  38.2 us (4%)
  between operations  21.9 us (2%)
    psum x1, waiting for transfers between devices, per_device(): summed = lax.psum(flat, ('group', 'member'))  491 us
    another operation x30, other arithmetic, per_device(): chols = [jnp.linalg.cholesky(fisher / total_rows + DAMP * eye)]  172 us
    another operation x4, other arithmetic, precondition(): whole = jax.scipy.linalg.solve_triangular(chol, half, lower=True, trans=1)  83.8 us
    all_to_all x2, waiting for transfers between devices, per_device(): lax.all_to_all(pieces, 'member', split_axis=1, concat_axis=1, tiled=True)  64.1 us
    all_to_all x2, waiting for transfers between devices, per_device(): lax.all_to_all(arrived, 'member', split_axis=1, concat_axis=1, tiled=True)  63.4 us
    another operation x14, matrix products, per_device(): chols = [jnp.linalg.cholesky(fisher / total_rows + DAMP * eye)]  23.1 us
    another operation x25, local copies, waits for them, and re-layouts  23 us
  transfers between devices with their start and end apart: 7, of which 7 were waited for; matrix products, arithmetic and copies ran while one was open for 1% of the time, Pallas kernels for 0%

commit v1 on v0

v1 whole, which is shorter than its diff:
```python
import functools
import math

import jax
import jax.numpy as jnp
from jax import lax
from jax.experimental import pallas as pl
from jax.experimental.pallas import tpu as pltpu
from jax.sharding import PartitionSpec as P

HI = lax.Precision.HIGHEST
NB = 8
B = 128

def dot(a, b, dims, precision=None):
    return lax.dot_general(a, b, (dims, ((), ())), precision=precision, preferred_element_type=jnp.float32)

def invert128(block):
    lane = lax.broadcasted_iota(jnp.int32, (8, B), 1)
    sub = lax.broadcasted_iota(jnp.int32, (8, B), 0)
    low = lane < 8
    unit = jnp.where(lane == sub, 1.0, 0.0).astype(jnp.float32)
    full = lambda v: jnp.broadcast_to(v, (8, B))
    rows = tuple(block[8 * i : 8 * i + 8] for i in range(16))
    first = tuple(full(rows[0][:, c : c + 1]) for c in range(8))

    def step(_, carry):
        a, cols = carry[:16], list(carry[16:])
        work = jnp.where(low, unit, a[0])
        for p in range(8):
            here = sub == p
            r = 1.0 / full(cols[p][p : p + 1])
            m = jnp.where(here, -r, cols[p] * r)
            for c in range(p + 1, 8):
                cols[c] = jnp.where(here, 0.0, cols[c]) - m * full(cols[c][p : p + 1])
            work = jnp.where(here, 0.0, work) - m * full(work[p : p + 1])
        wrow = [full(work[c : c + 1]) for c in range(8)]
        new = []
        for i in range(1, 16):
            t = [full(a[i][:, c : c + 1]) * wrow[c] for c in range(8)]
            s = ((t[0] + t[1]) + (t[2] + t[3])) + ((t[4] + t[5]) + (t[6] + t[7]))
            new.append(jnp.where(low, 0.0, a[i]) - s)
        new.append(work)
        nxt = tuple(full(new[0][:, 8 + c : 9 + c]) for c in range(8))
        return tuple(pltpu.roll(v, B - 8, 1) for v in new) + nxt

    out = lax.fori_loop(0, 16, step, rows + first)
    return jnp.concatenate(out[:16], axis=0)

def off(j):
    return sum((NB - t) * B for t in range(j))

def offg(j):
    return sum((NB - t) * B + 256 for t in range(j))

def kernel(below_ref, f_ref, g_ref, p0_ref, p1_ref, tiles_ref, scores_ref, a_ref, m_ref, x_ref, *, rows_all):
    eye = (lax.broadcasted_iota(jnp.int32, (B, B), 0) == lax.broadcasted_iota(jnp.int32, (B, B), 1)).astype(jnp.float32)
    for j in range(NB):
        n = (NB - j) * B
        a_ref[offg(j) : offg(j) + n] = f_ref[off(j) : off(j) + n] * (1.0 / rows_all)
        a_ref[offg(j) : offg(j) + B] += eye
        a_ref[offg(j) + n : offg(j) + n + 256] = g_ref[:, j * B : (j + 1) * B].astype(jnp.float32)
    for j in range(NB):
        o, n = offg(j), (NB - j) * B + 256
        inv = invert128(a_ref[o : o + B])
        m_ref[o + B : o + n] = dot(a_ref[o + B : o + n], inv, ((1,), (0,)), HI)
        for t in range(j + 1, NB):
            ot, nt = offg(t), (NB - t) * B + 256
            a_ref[ot : ot + nt] -= dot(m_ref[o + n - nt : o + n], a_ref[o + (t - j) * B : o + (t - j + 1) * B], ((1,), (1,)), HI)
    for j in reversed(range(NB)):
        o, n = offg(j), (NB - j) * B + 256
        z = m_ref[o + n - 256 : o + n]
        if j < NB - 1:
            z = z - dot(x_ref[:, (j + 1) * B :], m_ref[o + B : o + n - 256], ((1,), (0,)), HI)
        x_ref[:, j * B : (j + 1) * B] = z
    x = x_ref[...]
    hi = x.astype(jnp.bfloat16)
    lo = (x - hi.astype(jnp.float32)).astype(jnp.bfloat16)
    prod = hi.astype(jnp.float32) * g_ref[...].astype(jnp.float32)
    part = sum(prod[:, j * B : (j + 1) * B] for j in range(NB))
    scores_ref[...] = jnp.sum(part.T, axis=0, keepdims=True) * (1.0 / (NB * B))
    scale = 1.0 / math.sqrt(NB * B)
    for r, other in enumerate((p0_ref, p1_ref)):
        rest = jnp.where(below_ref[r] != 0, jnp.zeros_like(lo), lo)
        tiles_ref[r] = (dot(hi, other[...], ((1,), (1,))) + dot(rest, other[...], ((1,), (1,)))) * scale

def finish(below, f, g, p0, p1, rows_all):
    vm = pl.BlockSpec(memory_space=pltpu.VMEM)
    return pl.pallas_call(
        functools.partial(kernel, rows_all=rows_all),
        out_shape=(jax.ShapeDtypeStruct((2, 256, 256), jnp.float32), jax.ShapeDtypeStruct((1, 256), jnp.float32)),
        in_specs=[pl.BlockSpec(memory_space=pltpu.SMEM), vm, vm, vm, vm],
        out_specs=(vm, vm),
        scratch_shapes=[
            pltpu.VMEM((offg(NB), B), jnp.float32),
            pltpu.VMEM((offg(NB), B), jnp.float32),
            pltpu.VMEM((256, NB * B), jnp.float32),
        ],
        compiler_params=pltpu.CompilerParams(vmem_limit_bytes=48 << 20),
    )(below, f, g, p0, p1)


MESH = pl.DeviceIdType.MESH
TOTAL = NB * (NB + 1) // 2 * B
HALF = TOTAL // 2
PLANE = 16
SHARD = HALF // PLANE
DEPTH = 16
UNIT = 16
OWNERS = SHARD // UNIT


def place(x, y, z, core):
    return (lax.rem(y, 2) * 4 + x, z * 4 + lax.div(y, 2) * 2 + core)


def reduce_kernel(g_ref, f_ref, v_ref, gt_ref, s1, r1, s2, r2, w_ref, r3,
                  s1_sem, r1_sem, s2_sem, r2_sem, s3_sem, r3_sem, s4_sem, r4_sem, s5_sem, r5_sem, s6_sem, r6_sem):
    group, member = lax.axis_index("group"), lax.axis_index("member")
    x, y = lax.rem(group, 4), lax.div(group, 4) + 2 * lax.rem(lax.div(member, 2), 2)
    z, core = lax.div(member, 4), lax.rem(member, 2)
    spot = x * 4 + y

    def in_plane(s):
        return place(lax.div(s, 4), lax.rem(s, 4), z, core)

    def peer(k):
        return lax.rem(spot + k, PLANE)

    def on_column(other):
        return place(x, y, other, core)

    twin = place(x, y, z, 1 - core)

    def send(src, dst, ssem, rsem, dev):
        return pltpu.make_async_remote_copy(
            src_ref=src, dst_ref=dst, send_sem=ssem, recv_sem=rsem, device_id=dev, device_id_type=MESH
        )

    barrier = pltpu.get_barrier_semaphore()
    pl.semaphore_signal(barrier, inc=1, device_id=twin, device_id_type=MESH)
    for k in range(1, PLANE):
        pl.semaphore_signal(barrier, inc=1, device_id=in_plane(peer(k)), device_id_type=MESH)
    for k in range(1, DEPTH):
        pl.semaphore_signal(barrier, inc=1, device_id=on_column(lax.rem(z + k, DEPTH)), device_id_type=MESH)

    gt_ref[...] = g_ref[...].T
    for j in range(NB):
        v_ref[off(j) : off(j + 1)] = dot(gt_ref[j * B :], g_ref[:, j * B : (j + 1) * B], ((1,), (0,)))
    mine = pl.multiple_of(core * HALF, SHARD)
    theirs = pl.multiple_of((1 - core) * HALF, SHARD)
    s1[...] = v_ref[pl.ds(theirs, HALF)].astype(jnp.bfloat16)
    pl.semaphore_wait(barrier, PLANE + DEPTH - 1)

    c1 = send(s1, r1, s1_sem, r1_sem, twin)
    c1.start()
    c1.wait_recv()

    def shard(s):
        return pl.multiple_of(s * SHARD, SHARD)

    c2 = []
    for k in range(1, PLANE):
        s = peer(k)
        s2[k] = (v_ref[pl.ds(mine + shard(s), SHARD)] + r1[pl.ds(shard(s), SHARD)].astype(jnp.float32)).astype(jnp.bfloat16)
        c2.append(send(s2.at[k], r2.at[k], s2_sem.at[k], r2_sem.at[k], in_plane(s)))
        c2[-1].start()
    total = v_ref[pl.ds(mine + shard(spot), SHARD)] + r1[pl.ds(shard(spot), SHARD)].astype(jnp.float32)
    for k in range(1, PLANE):
        c2[k - 1].wait_recv()
        total += r2[k].astype(jnp.float32)
    w_ref[...] = total

    here = mine + shard(spot)

    def c3(u):
        k = lax.rem(u - z + DEPTH, DEPTH)
        return send(w_ref.at[pl.ds(u * UNIT, UNIT)], r3.at[k], s3_sem.at[u], r3_sem.at[k], on_column(u))

    def out_rows(u):
        return f_ref.at[pl.ds(pl.multiple_of(here + u * UNIT, UNIT), UNIT)]

    for u in range(OWNERS):
        @pl.when(z != u)
        def _(u=u):
            c3(u).start()

    @pl.when(z < OWNERS)
    def _():
        unit = w_ref[pl.ds(pl.multiple_of(z * UNIT, UNIT), UNIT)]
        for k in range(1, DEPTH):
            send(w_ref.at[pl.ds(0, UNIT)], r3.at[k], s3_sem.at[0], r3_sem.at[k], twin).wait_recv()
            unit += r3[k]
        f_ref[pl.ds(pl.multiple_of(here + z * UNIT, UNIT), UNIT)] = unit
        for k in range(1, DEPTH):
            send(out_rows(z), out_rows(z), s4_sem.at[k], r4_sem.at[z], on_column(lax.rem(z + k, DEPTH))).start()

    for u in range(OWNERS):
        @pl.when(z != u)
        def _(u=u):
            send(out_rows(u), out_rows(u), s4_sem.at[0], r4_sem.at[u], twin).wait_recv()

    def rows_of(s, half):
        return f_ref.at[pl.ds(pl.multiple_of(half + shard(s), SHARD), SHARD)]

    c6 = [send(rows_of(spot, mine), rows_of(spot, mine), s6_sem.at[0], r6_sem.at[0], twin)]
    c6[0].start()
    c5 = []
    for k in range(1, PLANE):
        c5.append(send(rows_of(spot, mine), rows_of(spot, mine), s5_sem.at[k], r5_sem.at[k], in_plane(peer(k))))
        c5[-1].start()
    for k in range(1, PLANE):
        s = peer(PLANE - k)
        send(rows_of(s, mine), rows_of(s, mine), s5_sem.at[k], r5_sem.at[k], twin).wait_recv()
        c6.append(send(rows_of(s, mine), rows_of(s, mine), s6_sem.at[k], r6_sem.at[k], twin))
        c6[-1].start()
    for k in range(PLANE):
        s = peer(PLANE - k)
        send(rows_of(s, theirs), rows_of(s, theirs), s6_sem.at[k], r6_sem.at[k], twin).wait_recv()

    c1.wait_send()
    for c in c2 + c5 + c6:
        c.wait_send()
    for u in range(OWNERS):
        @pl.when(z != u)
        def _(u=u):
            c3(u).wait_send()

    @pl.when(z < OWNERS)
    def _():
        for k in range(1, DEPTH):
            send(out_rows(z), out_rows(z), s4_sem.at[k], r4_sem.at[z], twin).wait_send()


def fisher_sum(block):
    vm = pl.BlockSpec(memory_space=pltpu.VMEM)
    sems = lambda *n: pltpu.SemaphoreType.DMA(n)
    return pl.pallas_call(
        reduce_kernel,
        out_shape=jax.ShapeDtypeStruct((TOTAL, B), jnp.float32),
        in_specs=[vm],
        out_specs=vm,
        scratch_shapes=[
            pltpu.VMEM((TOTAL, B), jnp.float32),
            pltpu.VMEM((NB * B, 256), jnp.bfloat16),
            pltpu.VMEM((HALF, B), jnp.bfloat16),
            pltpu.VMEM((HALF, B), jnp.bfloat16),
            pltpu.VMEM((PLANE, SHARD, B), jnp.bfloat16),
            pltpu.VMEM((PLANE, SHARD, B), jnp.bfloat16),
            pltpu.VMEM((SHARD, B), jnp.float32),
            pltpu.VMEM((DEPTH, UNIT, B), jnp.float32),
            pltpu.SemaphoreType.DMA, pltpu.SemaphoreType.DMA,
            sems(PLANE), sems(PLANE), sems(DEPTH), sems(DEPTH), sems(DEPTH), sems(DEPTH),
            sems(PLANE), sems(PLANE), sems(PLANE), sems(PLANE),
        ],
        compiler_params=pltpu.CompilerParams(collective_id=0, has_side_effects=True, vmem_limit_bytes=48 << 20),
    )(block)


def exchange(block, member_partner, group_partner):
    rows, width = block.shape
    members, groups = lax.axis_size("member"), lax.axis_size("group")
    group_here = lax.axis_index("group")
    partner_groups = group_partner[jnp.arange(groups, dtype=jnp.int32) * members] // members
    other_group = partner_groups[group_here]
    source_members = (
        lax.dynamic_slice(group_partner, (group_here * members,), (members,)) % members
    )
    spread = lax.all_to_all(
        block.reshape(members, rows // members, width), "member", split_axis=0, concat_axis=0, tiled=True
    )
    first = lax.all_to_all(
        jnp.take(spread, member_partner, axis=0), "member", split_axis=0, concat_axis=0, tiled=True
    ).reshape(rows, width)
    pieces = spread.reshape(groups, rows // groups, width)
    pieces = lax.all_to_all(pieces, "group", split_axis=0, concat_axis=0, tiled=True)
    pieces = lax.all_to_all(
        jnp.take(pieces, partner_groups, axis=0), "group", split_axis=0, concat_axis=0, tiled=True
    ).reshape(members, rows // members, width)
    second = lax.all_to_all(
        jnp.take(pieces, source_members, axis=0), "member", split_axis=0, concat_axis=0, tiled=True
    ).reshape(rows, width)
    return first, second


def per_device(grads, member_partner, group_partner):
    block = grads[0]
    rows_all = block.shape[0] * lax.axis_size("member") * lax.axis_size("group")
    member_here = lax.axis_index("member")
    block_here = lax.axis_index("group") * lax.axis_size("member") + member_here
    below = jnp.stack(
        [member_here < member_partner[member_here], block_here < group_partner[block_here]]
    ).astype(jnp.int32)
    first, second = exchange(block, member_partner, group_partner)
    fisher = fisher_sum(block)
    tiles, scores = finish(below, fisher, block, first, second, rows_all)
    return (tiles, scores.reshape(-1))


def solution(mesh):
    return jax.shard_map(
        per_device,
        mesh=mesh,
        in_specs=(P(None, ("group", "member"), None), P(), P()),
        out_specs=(P(None, ("group", "member"), None), P(("group", "member"))),
        check_vma=False,
    )
```

time: 1080 us -> 270 us (0.25)
  waiting for transfers between devices: 634 us -> 83.1 us
  other arithmetic: 276 us -> 3.4 us
  Pallas kernels: 0 us -> 128 us
  local copies, waits for them, and re-layouts: 59.2 us -> 11.7 us
  matrix products: 40.6 us -> 0 us
  between operations: 21.9 us -> 2.14 us
    psum x1 -> x0, waiting for transfers between devices: 491 us -> none  [per_device(): summed = lax.psum(flat, ('group', 'member'))]
    another operation x35 -> x0, other arithmetic: 257 us -> none  [the longest x30 172 us: per_device(): chols = [jnp.linalg.cholesky(fisher / total_rows + DAMP * eye)]]
    pallas_call x0 -> x2, Pallas kernels: none -> 128 us  [the longest x1 67.4 us: finish(): pl.pallas_call(functools.partial(kernel, rows_all=rows_all), out_shape=(j...]
    all_to_all x6 -> x5, waiting for transfers between devices: 144 us -> 83.1 us  [the longest x1 33.3 us: exchange(): lax.all_to_all(block.reshape(members, rows // members, width), 'member',...]
    another operation x44 -> x0, matrix products: 37.9 us -> none  [the longest x14 23.1 us: per_device(): chols = [jnp.linalg.cholesky(fisher / total_rows + DAMP * eye)]]
    another operation x38 -> x1, local copies, waits for them, and re-layouts: 26.4 us -> 2.04 us  [exchange(): block.reshape(members, rows // members, width)]
    all_to_all x6 -> x5, starting transfers between devices: 38.1 us -> 38.4 us  [the longest x1 19.8 us: exchange(): lax.all_to_all(block.reshape(members, rows // members, width), 'member',...]
  transfers between devices with their start and end apart: 7 -> 5, of which waited for: 7 -> 4; matrix products, arithmetic and copies ran while one was open for 1% -> 3% of each run, Pallas kernels for 0% -> 23%
where the time goes in v1:
time: 270 us; the launch traced here: 267 us
  Pallas kernels  128 us (47%)
  waiting for transfers between devices  83.1 us (31%)
  starting transfers between devices  38.4 us (14%)
  local copies, waits for them, and re-layouts  11.7 us (4%)
  other arithmetic  3.4 us (1%)
    pallas_call x1, Pallas kernels, finish(): pl.pallas_call(functools.partial(kernel, rows_all=rows_all), out_shape=(j...  67.4 us
    pallas_call x1, Pallas kernels, fisher_sum(): pl.pallas_call(reduce_kernel, out_shape=jax.ShapeDtypeStruct((TOTAL, B),...  60.6 us
    all_to_all x1, waiting for transfers between devices, exchange(): lax.all_to_all(block.reshape(members, rows // members, width), 'member',...  33.3 us
    all_to_all x1, waiting for transfers between devices, exchange(): lax.all_to_all(jnp.take(spread, member_partner, axis=0), 'member', split_...  31.5 us
    all_to_all x1, starting transfers between devices, exchange(): lax.all_to_all(block.reshape(members, rows // members, width), 'member',...  19.8 us
    all_to_all x1, waiting for transfers between devices, exchange(): lax.all_to_all(pieces, 'group', split_axis=0, concat_axis=0, tiled=True)  10.2 us
    all_to_all x1, waiting for transfers between devices, exchange(): lax.all_to_all(jnp.take(pieces, partner_groups, axis=0), 'group', split_a...  8.01 us
    all_to_all x1, starting transfers between devices, exchange(): lax.all_to_all(jnp.take(spread, member_partner, axis=0), 'member', split_...  5.88 us
  transfers between devices with their start and end apart: 5, of which 4 were waited for; matrix products, arithmetic and copies ran while one was open for 3% of the time, Pallas kernels for 23%

profile of v1, /device:TPU:1, one launch (start us, length us, event | category | flops | bytes accessed | tf_op | source)
XLA Modules:
  0.0 266.7 jit_solution(1843801390503719726)
XLA Ops:
  0.6 2.0 reshape_squeeze.3
  2.7 19.8 %all-to-all-start = ((bf16[64,4,1024]{2,1,0:T(4,128)(2,1)}), bf16[64,4,1024]{2,1,0:T(4,128)(2,1)S(1)}, u32[]{:S(2)}, u32[]{:S(2)}) async-start(bf16[64,4,1024]{2,1,0:T(4,128)(2,1)} %reshape_squeeze.3), calls=%async_computation | async-start | bytes 1048576 | tf_op jit(solution)/shard_map/all_to_all | solution.py:269
  22.5 0.6 gather_fusion
  23.2 33.3 %all-to-all-done = bf16[64,4,1024]{2,1,0:T(4,128)(2,1)S(1)} async-done(((bf16[64,4,1024]{2,1,0:T(4,128)(2,1)}), bf16[64,4,1024]{2,1,0:T(4,128)(2,1)S(1)}, u32[]{:S(2)}, u32[]{:S(2)}) %all-to-all-start) | async-done | bytes 524320 | tf_op jit(solution)/shard_map/all_to_all | solution.py:269
  56.5 0.9 reshape.104
  57.4 4.1 %all-to-all-start.2 = ((bf16[8,32,1024]{2,1,0:T(8,128)(2,1)}), bf16[8,32,1024]{2,1,0:T(8,128)(2,1)S(1)}, u32[]{:S(2)}, u32[]{:S(2)}) async-start(bf16[8,32,1024]{2,1,0:T(8,128)(2,1)} %reshape.104), calls=%async_computation.2 | async-start | bytes 1048576 | tf_op jit(solution)/shard_map/all_to_all | solution.py:276
  61.6 10.2 %all-to-all-done.2 = bf16[8,32,1024]{2,1,0:T(8,128)(2,1)S(1)} async-done(((bf16[8,32,1024]{2,1,0:T(8,128)(2,1)}), bf16[8,32,1024]{2,1,0:T(8,128)(2,1)S(1)}, u32[]{:S(2)}, u32[]{:S(2)}) %all-to-all-start.2) | async-done | bytes 524320 | tf_op jit(solution)/shard_map/all_to_all | solution.py:276
  72.4 0.9 broadcast_select_fusion.2
  73.3 3.5 %all-to-all-start.3 = ((bf16[8,32,1024]{2,1,0:T(8,128)(2,1)}), bf16[8,32,1024]{2,1,0:T(8,128)(2,1)S(1)}, u32[]{:S(2)}, u32[]{:S(2)}) async-start(bf16[8,32,1024]{2,1,0:T(8,128)(2,1)} %broadcast_select_fusion.2), calls=%async_computation.3 | async-start | bytes 1048576 | tf_op jit(solution)/shard_map/all_to_all | solution.py:277
  76.8 1.0 gather_fusion.2
  77.8 1.1 broadcast_select_fusion.1
  78.9 8.0 %all-to-all-done.3 = bf16[8,32,1024]{2,1,0:T(8,128)(2,1)S(1)} async-done(((bf16[8,32,1024]{2,1,0:T(8,128)(2,1)}), bf16[8,32,1024]{2,1,0:T(8,128)(2,1)S(1)}, u32[]{:S(2)}, u32[]{:S(2)}) %all-to-all-start.3) | async-done | bytes 524320 | tf_op jit(solution)/shard_map/all_to_all | solution.py:277
  86.9 5.9 %all-to-all-start.1 = ((bf16[64,4,1024]{2,1,0:T(4,128)(2,1)}), bf16[64,4,1024]{2,1,0:T(4,128)(2,1)S(1)}, u32[]{:S(2)}, u32[]{:S(2)}) async-start(bf16[64,4,1024]{2,1,0:T(4,128)(2,1)} %broadcast_select_fusion.1), calls=%async_computation.1 | async-start | bytes 1048576 | tf_op jit(solution)/shard_map/all_to_all | solution.py:272
  93.2 1.0 gather_fusion.3
  94.2 1.1 broadcast_select_fusion
  95.3 31.5 %all-to-all-done.1 = bf16[64,4,1024]{2,1,0:T(4,128)(2,1)S(1)} async-done(((bf16[64,4,1024]{2,1,0:T(4,128)(2,1)}), bf16[64,4,1024]{2,1,0:T(4,128)(2,1)S(1)}, u32[]{:S(2)}, u32[]{:S(2)}) %all-to-all-start.1) | async-done | bytes 524320 | tf_op jit(solution)/shard_map/all_to_all | solution.py:272
  126.8 5.1 %all-to-all-start.4 = ((bf16[64,4,1024]{2,1,0:T(4,128)(2,1)}), bf16[64,4,1024]{2,1,0:T(4,128)(2,1)}, u32[]{:S(2)}, u32[]{:S(2)}) async-start(bf16[64,4,1024]{2,1,0:T(4,128)(2,1)} %broadcast_select_fusion), calls=%async_computation.4 | async-start | bytes 1048576 | tf_op jit(solution)/shard_map/all_to_all | solution.py:280
  132.0 0.6 dynamic_slice.10
  133.2 0.6 dynamic_slice.9
  134.5 60.6 %shard_map.50.f_ref = f32[4608,128]{1,0:T(8,128)S(1)} custom-call(bf16[256,1024]{1,0:T(8,128)(2,1)S(1)} %bitcast.20), custom_call_target="tpu_custom_call" | custom-call | tf_op jit(solution)/shard_map/pallas_call | solution.py:238
  195.1 1.2 reshape.103.p0_ref
  196.3 2.0 reshape.106.p1_ref
  198.3 1.0 copy-done.1
  199.3 67.4 %shard_map.51 = (f32[2,256,256]{2,1,0:T(8,128)}, f32[1,256]{1,0:T(1,128)}) custom-call(s32[2]{0:T(128)S(1)} %add_convert_fusion.below_ref, f32[4608,128]{1,0:T(8,128)S(1)} %shard_map.50.f_ref, bf16[256,1024]{1,0:T(8,128)(2,1)S(1)} %bitcast.21, bf16[256,1024]{1,0:T(8,128)(2,1)S(1)} %reshape.103.p0_ref, bf16[256,1024]{1,0:T(8,128)(2,1)S(1)} %copy-done.1), custom_call_target="tpu_custom_call" | custom-call | tf_op jit(solution)/shard_map/pallas_call | solution.py:89
  (23 shorter events, 1.0 us)
Async XLA Ops:
  0.6 21.9 %copy-start.2 = (s32[512]{0:T(512)S(1)}, s32[512]{0:T(512)}, u32[]{:S(2)}) copy-start(s32[512]{0:T(512)} %param.7) | copy-start | bytes 6148
  0.6 22.5 %copy-start.4 = (s32[64]{0:T(128)S(1)}, s32[64]{0:T(128)}, u32[]{:S(2)}) copy-start(s32[64]{0:T(128)} %param.6) | copy-start | bytes 772
  2.7 53.8 %all-to-all-start = ((bf16[64,4,1024]{2,1,0:T(4,128)(2,1)}), bf16[64,4,1024]{2,1,0:T(4,128)(2,1)S(1)}, u32[]{:S(2)}, u32[]{:S(2)}) async-start(bf16[64,4,1024]{2,1,0:T(4,128)(2,1)} %reshape_squeeze.3), calls=%async_computation | async-start | bytes 1048576 | tf_op jit(solution)/shard_map/all_to_all | solution.py:269
  57.4 14.4 %all-to-all-start.2 = ((bf16[8,32,1024]{2,1,0:T(8,128)(2,1)}), bf16[8,32,1024]{2,1,0:T(8,128)(2,1)S(1)}, u32[]{:S(2)}, u32[]{:S(2)}) async-start(bf16[8,32,1024]{2,1,0:T(8,128)(2,1)} %reshape.104), calls=%async_computation.2 | async-start | bytes 1048576 | tf_op jit(solution)/shard_map/all_to_all | solution.py:276
  73.3 13.7 %all-to-all-start.3 = ((bf16[8,32,1024]{2,1,0:T(8,128)(2,1)}), bf16[8,32,1024]{2,1,0:T(8,128)(2,1)S(1)}, u32[]{:S(2)}, u32[]{:S(2)}) async-start(bf16[8,32,1024]{2,1,0:T(8,128)(2,1)} %broadcast_select_fusion.2), calls=%async_computation.3 | async-start | bytes 1048576 | tf_op jit(solution)/shard_map/all_to_all | solution.py:277
  86.9 39.9 %all-to-all-start.1 = ((bf16[64,4,1024]{2,1,0:T(4,128)(2,1)}), bf16[64,4,1024]{2,1,0:T(4,128)(2,1)S(1)}, u32[]{:S(2)}, u32[]{:S(2)}) async-start(bf16[64,4,1024]{2,1,0:T(4,128)(2,1)} %broadcast_select_fusion.1), calls=%async_computation.1 | async-start | bytes 1048576 | tf_op jit(solution)/shard_map/all_to_all | solution.py:272
  92.8 41.7 %copy-start = (bf16[1,256,1024]{2,1,0:T(8,128)(2,1)S(1)}, bf16[1,256,1024]{2,1,0:T(8,128)(2,1)}, u32[]{:S(2)}) copy-start(bf16[1,256,1024]{2,1,0:T(8,128)(2,1)} %param.5) | copy-start | bytes 1572868
  126.8 7.6 %copy-start.3 = (bf16[64,4,1024]{2,1,0:T(4,128)(2,1)}, bf16[64,4,1024]{2,1,0:T(4,128)(2,1)S(1)}, u32[]{:S(2)}) copy-start(bf16[64,4,1024]{2,1,0:T(4,128)(2,1)S(1)} %all-to-all-done.1) | copy-start | bytes 1572868
  126.8 69.5 %all-to-all-start.4 = ((bf16[64,4,1024]{2,1,0:T(4,128)(2,1)}), bf16[64,4,1024]{2,1,0:T(4,128)(2,1)}, u32[]{:S(2)}, u32[]{:S(2)}) async-start(bf16[64,4,1024]{2,1,0:T(4,128)(2,1)} %broadcast_select_fusion), calls=%async_computation.4 | async-start | bytes 1048576 | tf_op jit(solution)/shard_map/all_to_all | solution.py:280
  198.3 1.0 copy-start.1
